TPU v7x, 32 devices: a whole 2x2x4 slice. The times are simulated.
32 devices in a mesh: group: 2 (over x), tile: 16 (over z, y, core).
Axes of the slice: x: 2, y: 2, z: 4, core: 2. Of those that a mesh axis runs over, the one named last changes fastest.
Arguments:
- samples: bfloat16 [2, 1024, 65984], P(None, ('group', 'tile')), parts along dimension 1, may hold values from -6 to 6
- fir_taps: float32 [8, 64], replicated, may hold values from -2 to 2
- chan_map: int32 [32], replicated, may hold values from 0 to 63, as said below
- layout: int32 [10], replicated, may hold values from 0 to 9, each once
Outputs:
- visibilities: float32 [640, 2, 128, 128], P(('group', 'tile')), parts along dimension 0
There are 2 independent parts, one for each index of `group`. A program takes and returns all parts, laid end to end along the dimension named above; an argument that names none is the same for every part. Nothing has to cross between parts.
Inputs may be any that keep to these rules, and one draw needn't show every extreme that they name: `chan_map`: 32 distinct channels in increasing order; channels 0 and 63 are always kept. `layout`: each block pair once.
All inputs are finite; a program needn't handle non-finite values.
Results may differ from a plain program's by a relative error of at most 0.0033.
Values may be sent and summed in bfloat16 or wider, within the bound.
A program may use at most 128 MiB of HBM per device.

v0:
```python
import math
import jax
import jax.numpy as jnp
import numpy as np
from jax import lax
from jax.sharding import PartitionSpec as P

NCHAN = 64
KEEP = 32
TAPS = 8
BLOCK = 128
CH = 4
NBLK = 4
NPAIR = 10


def swapped_2(block, axis, stride):
    count = lax.axis_size(axis)
    route = []
    for low in range(count):
        high = low | 1 << stride
        if high != low and high < count:
            route += [(low, high), (high, low)]
    return lax.ppermute(block, axis, route)


def pair_tables(block_count):
    first_block = []
    second_block = []
    for i in range(block_count):
        for j in range(i, block_count):
            first_block.append(i)
            second_block.append(j)
    return (np.array(first_block, np.int32), np.array(second_block, np.int32))


def dft_table(channels):
    tap_index = jnp.arange(NCHAN, dtype=jnp.int32).reshape((NCHAN,) + (1,) * channels.ndim)
    phases = tap_index * channels[None] % NCHAN
    angles = phases.astype(jnp.float32) * (2.0 * math.pi / NCHAN)
    scaling = 1.0 / math.sqrt(NCHAN)
    cosine = jnp.cos(angles) * scaling
    sine_part = jnp.sin(angles) * scaling
    real_rows = jnp.stack([cosine, -sine_part], 1)
    imag_rows = jnp.stack([sine_part, cosine], 1)
    return jnp.stack([real_rows, imag_rows], 0).astype(jnp.bfloat16)


def weigh(samples, fir_taps, spec_count):
    summed = jnp.zeros(samples.shape[:2] + (spec_count * NCHAN,), jnp.float32)
    for k in range(TAPS):
        window = lax.slice_in_dim(
            samples, k * NCHAN, k * NCHAN + spec_count * NCHAN, axis=2
        ).astype(jnp.float32)
        summed = summed + window * jnp.tile(fir_taps[k], spec_count)
    return summed.astype(jnp.bfloat16)


def lookup(positions, table_values):
    onehot = positions[:, None] == jnp.arange(table_values.shape[0], dtype=jnp.int32)[None, :]
    return jnp.sum(jnp.where(onehot, table_values[None, :], 0), 1).astype(jnp.int32)


def on_device(samples, fir_taps, chan_map, layout):
    tile_count = lax.axis_size("tile")
    in_dev = samples.shape[1]
    input_total = in_dev * tile_count
    spec_count = samples.shape[2] // NCHAN - TAPS + 1
    weighted = weigh(samples, fir_taps, spec_count)
    first_block, second_block = pair_tables(NBLK)
    first_table = jnp.asarray(first_block)
    second_table = jnp.asarray(second_block)
    tb_count = tile_count * CH // KEEP
    time_len = spec_count // tb_count
    first_sel = lookup(layout, first_table)
    second_sel = lookup(layout, second_table)
    dft_rows = dft_table(chan_map.reshape(KEEP // CH, CH))
    frames = weighted.reshape(2, in_dev, tb_count, time_len, NCHAN)
    spectra = jnp.einsum(
        "rnqoc,ribtn->obiqct", dft_rows, frames, preferred_element_type=jnp.float32
    )
    spectra = spectra.astype(jnp.bfloat16).reshape(tile_count, in_dev, 2, CH, time_len)
    received = lax.all_to_all(spectra, "tile", split_axis=0, concat_axis=1, tiled=True)
    c_items = received.shape[3]
    flat_inputs = received.reshape(input_total, 2, c_items, time_len)
    swapped = jnp.stack([-flat_inputs[:, 1], flat_inputs[:, 0]], 1)
    real_full = jnp.einsum(
        "apct,bpct->cab", flat_inputs, flat_inputs, preferred_element_type=jnp.float32
    )
    imag_full = jnp.einsum(
        "apct,bpct->cab", flat_inputs, swapped, preferred_element_type=jnp.float32
    )
    real_full = real_full.reshape(c_items, NBLK, BLOCK, NBLK, BLOCK)
    imag_full = imag_full.reshape(c_items, NBLK, BLOCK, NBLK, BLOCK)
    real_blocks = real_full[:, first_sel, :, second_sel, :]
    imag_blocks = imag_full[:, first_sel, :, second_sel, :]
    stacked = jnp.stack([real_blocks, imag_blocks], 2)
    partial_terms = jnp.swapaxes(stacked, 0, 1)
    row_terms = partial_terms.reshape(CH * NPAIR, 2, BLOCK, BLOCK)
    time_slot = lax.axis_index("tile") % tb_count
    level_count = tb_count.bit_length() - 1
    for bit_level in range(level_count - 1, -1, -1):
        half_rows = row_terms.shape[0] // 2
        upper_bit = time_slot // (1 << bit_level) % 2
        kept_rows = lax.dynamic_slice_in_dim(row_terms, upper_bit * half_rows, half_rows, 0)
        sent_rows = lax.dynamic_slice_in_dim(row_terms, (1 - upper_bit) * half_rows, half_rows, 0)
        row_terms = kept_rows + swapped_2(sent_rows, "tile", bit_level)
    return row_terms / spec_count


def solution(mesh):
    placed = (P(None, ("group", "tile"), None), P(), P(), P())
    return jax.shard_map(
        on_device,
        mesh=mesh,
        in_specs=placed,
        out_specs=P(("group", "tile"), None, None, None),
        check_vma=False,
    )
```

profile of v0, /device:TPU:17, one launch (start us, length us, event | category | flops | bytes accessed | tf_op | source)
XLA Modules:
  0.0 224.6 jit_solution(8689402433933781313)
XLA Ops:
  0.0 1.0 slice_bitcast_fusion.7
  2.5 34.4 %add_convert_fusion = bf16[2,32,65536]{2,1,0:T(8,128)(2,1)} fusion(f32[65536]{0:T(1024)S(1)} %mul.182, bf16[2,32,65984]{2,1,0:T(8,128)(2,1)} %param.6, f32[65536]{0:T(1024)S(1)} %mul.179, f32[65536]{0:T(1024)S(1)} %mul.176, f32[65536]{0:T(1024)S(1)} %mul.173, f32[65536]{0:T(1024)S(1)} %mul.170, f32[65536]{0:T(1024)S(1)} %mul.167, f32[65536]{0:T(1024)S(1)} %mul.164, ...), kind=kLoop, calls=%fused_computation.4 | loop fusion | flops 100663296 | bytes 77594624 | tf_op jit(solution)/shard_map/convert_element_type | solution.py:56
  36.9 18.2 %reshape.121 = bf16[2,32,2,512,64]{4,3,2,1,0:T(8,128)(2,1)} reshape(bf16[2,32,65536]{2,1,0:T(8,128)(2,1)} %add_convert_fusion) | data formatting | bytes 16777216 | tf_op jit(solution)/shard_map/reshape | solution.py:78
  55.4 10.9 %fusion.2 = bf16[8,2,32,2,4,512]{5,0,4,3,1,2:T(8,128)(2,1)S(1)} fusion(bf16[1,64,2,8,4]{1,3,0,4,2:T(8,128)(2,1)S(1)} %get-tuple-element.10, bf16[1,64,2,8,4]{1,3,0,4,2:T(8,128)(2,1)S(1)} %get-tuple-element.9, bf16[2,32,2,512,64]{4,3,2,1,0:T(8,128)(2,1)} %reshape.121), kind=kOutput, calls=%fused_computation.7 | convolution fusion | flops 539000832 | bytes 12599296 | tf_op jit(solution)/shard_map/rnqoc,ribtn->obiqct/dot_general | solution.py:79
  66.3 4.4 %copy.29 = bf16[8,2,32,2,4,512]{5,2,4,3,1,0:T(8,128)(2,1)} copy(bf16[8,2,32,2,4,512]{5,0,4,3,1,2:T(8,128)(2,1)S(1)} %fusion.2) | data formatting | bytes 8388608 | tf_op jit(solution)/shard_map/convert_element_type | solution.py:82
  70.7 6.6 %all-to-all-start = ((bf16[16,32,2,4,512]{4,1,3,2,0:T(8,128)(2,1)}), bf16[16,32,2,4,512]{4,1,3,2,0:T(8,128)(2,1)}, u32[]{:S(2)}, u32[]{:S(2)}) async-start(bf16[16,32,2,4,512]{4,1,3,2,0:T(8,128)(2,1)} %bitcast.66), calls=%async_computation | async-start | bytes 8388608 | tf_op jit(solution)/shard_map/all_to_all | solution.py:83
  77.5 92.0 %all-to-all-done = bf16[16,32,2,4,512]{4,1,3,2,0:T(8,128)(2,1)} async-done(((bf16[16,32,2,4,512]{4,1,3,2,0:T(8,128)(2,1)}), bf16[16,32,2,4,512]{4,1,3,2,0:T(8,128)(2,1)}, u32[]{:S(2)}, u32[]{:S(2)}) %all-to-all-start) | async-done | bytes 4194336 | tf_op jit(solution)/shard_map/all_to_all | solution.py:83
  169.5 2.5 %copy.30 = bf16[16,32,2,4,512]{4,1,0,2,3:T(8,128)(2,1)S(1)} copy(bf16[16,32,2,4,512]{4,1,3,2,0:T(8,128)(2,1)} %all-to-all-done) | data formatting | bytes 8388608 | tf_op jit(solution)/shard_map/all_to_all | solution.py:83
  172.0 0.3 slice_negate_fusion
  172.2 4.3 %convolution_bitcast_fusion = f32[4,512,512]{2,1,0:T(8,128)} fusion(bf16[512,2,4,512]{3,0,1,2:T(8,128)(2,1)S(1)} %bitcast.68), kind=kOutput, calls=%fused_computation.14 | convolution fusion | flops 2147483648 | bytes 8388608 | tf_op jit(solution)/shard_map/apct,bpct->cab/dot_general | solution.py:87
  176.6 4.4 %fusion.9 = f32[4,512,512]{2,1,0:T(8,128)} fusion(bf16[512,2,4,512]{3,0,1,2:T(8,128)(2,1)S(1)} %bitcast.69, bf16[512,1,4,512]{3,0,1,2:T(8,128)(2,1)S(1)} %get-tuple-element.8, bf16[512,1,4,512]{3,0,1,2:T(8,128)(2,1)S(1)} %get-tuple-element.7), kind=kOutput, calls=%fused_computation.13 | convolution fusion | flops 2149580800 | bytes 12582912 | tf_op jit(solution)/shard_map/apct,bpct->cab/dot_general | solution.py:90
  180.9 5.3 %reshape.125 = f32[4,4,128,4,128]{4,3,2,1,0:T(4,128)} reshape(f32[4,512,512]{2,1,0:T(8,128)} %fusion.9) | data formatting | bytes 8388608 | tf_op jit(solution)/shard_map/reshape | solution.py:94
  186.2 4.8 %copy.32 = f32[4,4,128,4,128]{4,2,3,1,0:T(8,128)} copy(f32[4,4,128,4,128]{4,3,2,1,0:T(4,128)} %reshape.125) | data formatting | bytes 8388608 | tf_op jit(solution)/shard_map/reshape | solution.py:94
  191.0 5.3 %reshape.124 = f32[4,4,128,4,128]{4,3,2,1,0:T(4,128)} reshape(f32[4,512,512]{2,1,0:T(8,128)} %convolution_bitcast_fusion) | data formatting | bytes 8388608 | tf_op jit(solution)/shard_map/reshape | solution.py:93
  196.2 4.7 %copy.31 = f32[4,4,128,4,128]{4,2,3,1,0:T(8,128)} copy(f32[4,4,128,4,128]{4,3,2,1,0:T(4,128)} %reshape.124) | data formatting | bytes 8388608 | tf_op jit(solution)/shard_map/reshape | solution.py:93
  201.0 2.9 %gather_fusion.1 = f32[10,4,128,128]{3,2,1,0:T(8,128)S(1)} fusion(f32[4,4,128,4,128]{4,2,3,1,0:T(8,128)} %copy.32, s32[10]{0:T(128)S(1)} %fusion.26), kind=kCustom, calls=%fused_computation.1 | custom fusion | bytes 5242960 | tf_op jit(solution)/shard_map/gather | solution.py:96
  203.9 4.5 %gather_fusion = f32[10,4,128,128]{3,2,1,0:T(8,128)} fusion(f32[4,4,128,4,128]{4,2,3,1,0:T(8,128)} %copy.31, s32[10]{0:T(128)S(1)} %fusion.26), kind=kCustom, calls=%fused_computation | custom fusion | bytes 5242960 | tf_op jit(solution)/shard_map/gather | solution.py:95
  208.4 2.2 maximum_bitcast_fusion
  210.6 0.6 copy.33
  211.2 2.3 %copy-done = f32[4,10,2,128,128]{4,3,2,1,0:T(8,128)} copy-done((f32[4,10,2,128,128]{4,3,2,1,0:T(8,128)}, f32[4,10,2,128,128]{4,3,2,1,0:T(8,128)S(1)}, u32[]{:S(2)}) %copy-start) | copy-done | bytes 5242904
  213.5 1.8 constant_dynamic-slice_fusion
  215.3 0.9 collective-permute-start
  216.2 4.7 %collective-permute-done = f32[20,2,128,128]{3,2,1,0:T(8,128)S(1)} collective-permute-done((f32[20,2,128,128]{3,2,1,0:T(8,128)}, f32[20,2,128,128]{3,2,1,0:T(8,128)S(1)}, u32[]{:S(2)}, u32[]{:S(2)}) %collective-permute-start) | collective-permute-done | bytes 2621472 | tf_op jit(solution)/shard_map/ppermute | solution.py:24
  220.9 3.7 %add_multiply_fusion = f32[20,2,128,128]{3,2,1,0:T(8,128)} fusion(f32[20,2,128,128]{3,2,1,0:T(8,128)S(1)} %collective-permute-done, f32[40,2,128,128]{3,2,1,0:T(8,128)} %bitcast.65, s32[]{:T(128)S(6)} %select_n.76), kind=kLoop, calls=%fused_computation.12 | loop fusion | flops 1310720 | bytes 7864324 | tf_op jit(solution)/shard_map/div | solution.py:108
  (31 shorter events, 1.9 us)
Async XLA Ops:
  36.9 18.2 %copy-start.1 = (s32[32]{0:T(128)S(1)}, s32[32]{0:T(128)}, u32[]{:S(2)}) copy-start(s32[32]{0:T(128)} %param.8) | copy-start | bytes 388
  70.6 6.6 %copy-start.2 = (s32[10]{0:T(128)S(1)}, s32[10]{0:T(128)}, u32[]{:S(2)}) copy-start(s32[10]{0:T(128)} %param.9) | copy-start | bytes 124
  70.7 6.6 %copy-start.3 = (s32[10]{0:T(128)S(1)}, s32[10]{0:T(128)}, u32[]{:S(2)}) copy-start(s32[10]{0:T(128)} %constant.65.clone) | copy-start | bytes 124
  70.7 6.7 %copy-start.4 = (s32[10]{0:T(128)S(1)}, s32[10]{0:T(128)}, u32[]{:S(2)}) copy-start(s32[10]{0:T(128)} %constant.66.clone) | copy-start | bytes 124
  70.7 98.8 %all-to-all-start = ((bf16[16,32,2,4,512]{4,1,3,2,0:T(8,128)(2,1)}), bf16[16,32,2,4,512]{4,1,3,2,0:T(8,128)(2,1)}, u32[]{:S(2)}, u32[]{:S(2)}) async-start(bf16[16,32,2,4,512]{4,1,3,2,0:T(8,128)(2,1)} %bitcast.66), calls=%async_computation | async-start | bytes 8388608 | tf_op jit(solution)/shard_map/all_to_all | solution.py:83
  211.2 2.3 %copy-start = (f32[4,10,2,128,128]{4,3,2,1,0:T(8,128)}, f32[4,10,2,128,128]{4,3,2,1,0:T(8,128)S(1)}, u32[]{:S(2)}) copy-start(f32[4,10,2,128,128]{4,3,2,1,0:T(8,128)S(1)} %copy.33) | copy-start | bytes 15728644
  215.3 5.6 %collective-permute-start = (f32[20,2,128,128]{3,2,1,0:T(8,128)}, f32[20,2,128,128]{3,2,1,0:T(8,128)S(1)}, u32[]{:S(2)}, u32[]{:S(2)}) collective-permute-start(f32[20,2,128,128]{3,2,1,0:T(8,128)} %constant_dynamic-slice_fusion), channel_id=1, source_target_pairs={{0,1},{1,0},{2,3},{3,2},{4,5},{5,4},{6,7},{7,6},{8,9},{9,8},{10,11... | collective-permute-start | bytes 7864328 | tf_op jit(solution)/shard_map/ppermute | solution.py:24
where the time goes:
time: 226 us; the launch traced here: 225 us
  waiting for transfers between devices  96.7 us (43%)
  local copies, waits for them, and re-layouts  59.7 us (26%)
  other arithmetic  40.9 us (18%)
  matrix products  19.5 us (9%)
  starting transfers between devices  7.49 us (3%)
    all_to_all x1, waiting for transfers between devices, on_device(): lax.all_to_all(spectra, 'tile', split_axis=0, concat_axis=1, tiled=True)  92 us
    convert_element_type x1, other arithmetic, weigh(): return summed.astype(jnp.bfloat16)  34.4 us
    reshape x1, local copies, waits for them, and re-layouts, on_device(): frames = weighted.reshape(2, in_dev, tb_count, time_len, NCHAN)  18.2 us
    dot_general x1, matrix products, on_device(): jnp.einsum('rnqoc,ribtn->obiqct', dft_rows, frames, preferred_element_typ...  10.9 us
    reshape x2, local copies, waits for them, and re-layouts, on_device(): imag_full = imag_full.reshape(c_items, NBLK, BLOCK, NBLK, BLOCK)  10.1 us
    reshape x2, local copies, waits for them, and re-layouts, on_device(): real_full = real_full.reshape(c_items, NBLK, BLOCK, NBLK, BLOCK)  10 us
    all_to_all x1, starting transfers between devices, on_device(): lax.all_to_all(spectra, 'tile', split_axis=0, concat_axis=1, tiled=True)  6.63 us
    ppermute x1, waiting for transfers between devices, swapped_2(): return lax.ppermute(block, axis, route)  4.75 us
  transfers between devices with their start and end apart: 2, of which 2 were waited for; matrix products, arithmetic and copies ran while one was open for 0% of the time, Pallas kernels for 0%

commit v1 on v0

--- a/solution.py
+++ b/solution.py
@@ -80,7 +80,10 @@
         "rnqoc,ribtn->obiqct", dft_rows, frames, preferred_element_type=jnp.float32
     )
     spectra = spectra.astype(jnp.bfloat16).reshape(tile_count, in_dev, 2, CH, time_len)
-    received = lax.all_to_all(spectra, "tile", split_axis=0, concat_axis=1, tiled=True)
+    received = jnp.concatenate(
+        lax.all_to_all(jnp.stack(jnp.split(spectra, lax.psum(1, "tile"), 0), axis=0), "tile", 0, 0),
+        1,
+    )
     c_items = received.shape[3]
     flat_inputs = received.reshape(input_total, 2, c_items, time_len)
     swapped = jnp.stack([-flat_inputs[:, 1], flat_inputs[:, 0]], 1)

time: 226 us -> 235 us (1.040)
  local copies, waits for them, and re-layouts: 59.7 us -> 69.3 us
    unnamed x10 -> x25, local copies, waits for them, and re-layouts: 2.31 us -> 13.2 us
where the time goes in v1:
time: 235 us; the launch traced here: 234 us
  waiting for transfers between devices  96.7 us (41%)
  local copies, waits for them, and re-layouts  69.3 us (29%)
  other arithmetic  40.9 us (17%)
  matrix products  19.5 us (8%)
  starting transfers between devices  7.49 us (3%)
    all_to_all x1, waiting for transfers between devices, on_device(): lax.all_to_all(jnp.stack(jnp.split(spectra, lax.psum(1, 'tile'), 0), axis...  92 us
    convert_element_type x1, other arithmetic, weigh(): return summed.astype(jnp.bfloat16)  34.4 us
    reshape x1, local copies, waits for them, and re-layouts, on_device(): frames = weighted.reshape(2, in_dev, tb_count, time_len, NCHAN)  18.2 us
    unnamed x25, local copies, waits for them, and re-layouts  13.2 us
    dot_general x1, matrix products, on_device(): jnp.einsum('rnqoc,ribtn->obiqct', dft_rows, frames, preferred_element_typ...  10.9 us
    reshape x2, local copies, waits for them, and re-layouts, on_device(): imag_full = imag_full.reshape(c_items, NBLK, BLOCK, NBLK, BLOCK)  10.1 us
    reshape x2, local copies, waits for them, and re-layouts, on_device(): real_full = real_full.reshape(c_items, NBLK, BLOCK, NBLK, BLOCK)  10 us
    all_to_all x1, starting transfers between devices, on_device(): lax.all_to_all(jnp.stack(jnp.split(spectra, lax.psum(1, 'tile'), 0), axis...  6.63 us
  transfers between devices with their start and end apart: 2, of which 2 were waited for; matrix products, arithmetic and copies ran while one was open for 0% of the time, Pallas kernels for 0%

profile of v1, /device:TPU:17, one launch (start us, length us, event | category | flops | bytes accessed | tf_op | source)
XLA Modules:
  0.0 234.2 jit_solution(11052370513527778253)
XLA Ops:
  0.0 1.0 slice_bitcast_fusion.23
  2.5 34.4 %add_convert_fusion = bf16[2,32,65536]{2,1,0:T(8,128)(2,1)} fusion(f32[65536]{0:T(1024)S(1)} %mul.182, bf16[2,32,65984]{2,1,0:T(8,128)(2,1)} %param.6, f32[65536]{0:T(1024)S(1)} %mul.179, f32[65536]{0:T(1024)S(1)} %mul.176, f32[65536]{0:T(1024)S(1)} %mul.173, f32[65536]{0:T(1024)S(1)} %mul.170, f32[65536]{0:T(1024)S(1)} %mul.167, f32[65536]{0:T(1024)S(1)} %mul.164, ...), kind=kLoop, calls=%fused_computation.4 | loop fusion | flops 100663296 | bytes 77594624 | tf_op jit(solution)/shard_map/convert_element_type | solution.py:56
  36.9 18.2 %reshape.114 = bf16[2,32,2,512,64]{4,3,2,1,0:T(8,128)(2,1)} reshape(bf16[2,32,65536]{2,1,0:T(8,128)(2,1)} %add_convert_fusion) | data formatting | bytes 16777216 | tf_op jit(solution)/shard_map/reshape | solution.py:78
  55.4 10.9 %fusion.2 = bf16[8,2,32,2,4,512]{5,0,4,3,1,2:T(8,128)(2,1)S(1)} fusion(bf16[1,64,2,8,4]{1,3,0,4,2:T(8,128)(2,1)S(1)} %get-tuple-element.10, bf16[1,64,2,8,4]{1,3,0,4,2:T(8,128)(2,1)S(1)} %get-tuple-element.9, bf16[2,32,2,512,64]{4,3,2,1,0:T(8,128)(2,1)} %reshape.114), kind=kOutput, calls=%fused_computation.7 | convolution fusion | flops 539000832 | bytes 12599296 | tf_op jit(solution)/shard_map/rnqoc,ribtn->obiqct/dot_general | solution.py:79
  66.3 2.4 %copy.44 = bf16[8,2,32,2,4,512]{5,2,4,3,1,0:T(8,128)(2,1)S(1)} copy(bf16[8,2,32,2,4,512]{5,0,4,3,1,2:T(8,128)(2,1)S(1)} %fusion.2) | data formatting | bytes 8388608 | tf_op jit(solution)/shard_map/convert_element_type | solution.py:82
  70.1 0.7 fusion.25
  79.5 0.8 fusion.12
  80.3 6.6 %all-to-all-start = ((bf16[16,1,32,2,4,512]{5,2,4,3,1,0:T(8,128)(2,1)}), bf16[16,1,32,2,4,512]{5,2,4,3,1,0:T(8,128)(2,1)}, u32[]{:S(2)}, u32[]{:S(2)}) async-start(bf16[16,1,32,2,4,512]{5,2,4,3,1,0:T(8,128)(2,1)} %fusion.12), calls=%async_computation | async-start | bytes 8388608 | tf_op jit(solution)/shard_map/all_to_all | solution.py:84
  87.1 92.0 %all-to-all-done = bf16[16,1,32,2,4,512]{5,2,4,3,1,0:T(8,128)(2,1)} async-done(((bf16[16,1,32,2,4,512]{5,2,4,3,1,0:T(8,128)(2,1)}), bf16[16,1,32,2,4,512]{5,2,4,3,1,0:T(8,128)(2,1)}, u32[]{:S(2)}, u32[]{:S(2)}) %all-to-all-start) | async-done | bytes 4194336 | tf_op jit(solution)/shard_map/all_to_all | solution.py:84
  179.1 2.5 %copy.45 = bf16[16,1,32,2,4,512]{5,2,0,3,4,1:T(8,128)(2,1)S(1)} copy(bf16[16,1,32,2,4,512]{5,2,4,3,1,0:T(8,128)(2,1)} %all-to-all-done) | data formatting | bytes 8388608 | tf_op jit(solution)/shard_map/all_to_all | solution.py:84
  181.9 4.3 %convolution_bitcast_fusion = f32[4,512,512]{2,1,0:T(8,128)} fusion(bf16[512,2,4,512]{3,0,1,2:T(8,128)(2,1)S(1)} %bitcast.147), kind=kOutput, calls=%fused_computation.14 | convolution fusion | flops 2147483648 | bytes 8388608 | tf_op jit(solution)/shard_map/apct,bpct->cab/dot_general | solution.py:90
  186.2 4.4 %fusion.9 = f32[4,512,512]{2,1,0:T(8,128)} fusion(bf16[512,2,4,512]{3,0,1,2:T(8,128)(2,1)S(1)} %bitcast.148, bf16[512,1,4,512]{3,0,1,2:T(8,128)(2,1)S(1)} %get-tuple-element.8, bf16[512,1,4,512]{3,0,1,2:T(8,128)(2,1)S(1)} %get-tuple-element.7), kind=kOutput, calls=%fused_computation.13 | convolution fusion | flops 2149580800 | bytes 12582912 | tf_op jit(solution)/shard_map/apct,bpct->cab/dot_general | solution.py:93
  190.5 5.3 %reshape.117 = f32[4,4,128,4,128]{4,3,2,1,0:T(4,128)} reshape(f32[4,512,512]{2,1,0:T(8,128)} %fusion.9) | data formatting | bytes 8388608 | tf_op jit(solution)/shard_map/reshape | solution.py:97
  195.8 4.8 %copy.47 = f32[4,4,128,4,128]{4,2,3,1,0:T(8,128)} copy(f32[4,4,128,4,128]{4,3,2,1,0:T(4,128)} %reshape.117) | data formatting | bytes 8388608 | tf_op jit(solution)/shard_map/reshape | solution.py:97
  200.6 5.3 %reshape.116 = f32[4,4,128,4,128]{4,3,2,1,0:T(4,128)} reshape(f32[4,512,512]{2,1,0:T(8,128)} %convolution_bitcast_fusion) | data formatting | bytes 8388608 | tf_op jit(solution)/shard_map/reshape | solution.py:96
  205.9 4.7 %copy.46 = f32[4,4,128,4,128]{4,2,3,1,0:T(8,128)} copy(f32[4,4,128,4,128]{4,3,2,1,0:T(4,128)} %reshape.116) | data formatting | bytes 8388608 | tf_op jit(solution)/shard_map/reshape | solution.py:96
  210.6 2.9 %gather_fusion.1 = f32[10,4,128,128]{3,2,1,0:T(8,128)S(1)} fusion(f32[4,4,128,4,128]{4,2,3,1,0:T(8,128)} %copy.47, s32[10]{0:T(128)S(1)} %fusion.42), kind=kCustom, calls=%fused_computation.1 | custom fusion | bytes 5242960 | tf_op jit(solution)/shard_map/gather | solution.py:99
  213.5 4.5 %gather_fusion = f32[10,4,128,128]{3,2,1,0:T(8,128)} fusion(f32[4,4,128,4,128]{4,2,3,1,0:T(8,128)} %copy.46, s32[10]{0:T(128)S(1)} %fusion.42), kind=kCustom, calls=%fused_computation | custom fusion | bytes 5242960 | tf_op jit(solution)/shard_map/gather | solution.py:98
  218.0 2.2 maximum_bitcast_fusion
  220.9 2.3 copy-done
  223.1 1.8 constant_dynamic-slice_fusion
  224.9 0.9 collective-permute-start
  225.8 4.7 %collective-permute-done = f32[20,2,128,128]{3,2,1,0:T(8,128)S(1)} collective-permute-done((f32[20,2,128,128]{3,2,1,0:T(8,128)}, f32[20,2,128,128]{3,2,1,0:T(8,128)S(1)}, u32[]{:S(2)}, u32[]{:S(2)}) %collective-permute-start) | collective-permute-done | bytes 2621472 | tf_op jit(solution)/shard_map/ppermute | solution.py:24
  230.5 3.7 %add_multiply_fusion = f32[20,2,128,128]{3,2,1,0:T(8,128)} fusion(f32[20,2,128,128]{3,2,1,0:T(8,128)S(1)} %collective-permute-done, f32[40,2,128,128]{3,2,1,0:T(8,128)} %bitcast.129, s32[]{:T(128)S(6)} %select_n.76), kind=kLoop, calls=%fused_computation.12 | loop fusion | flops 1310720 | bytes 7864324 | tf_op jit(solution)/shard_map/div | solution.py:111
  (47 shorter events, 12.9 us)
Async XLA Ops:
  36.9 18.2 %copy-start.1 = (s32[32]{0:T(128)S(1)}, s32[32]{0:T(128)}, u32[]{:S(2)}) copy-start(s32[32]{0:T(128)} %param.8) | copy-start | bytes 388
  80.3 6.6 %copy-start.2 = (s32[10]{0:T(128)S(1)}, s32[10]{0:T(128)}, u32[]{:S(2)}) copy-start(s32[10]{0:T(128)} %param.9) | copy-start | bytes 124
  80.3 6.6 %copy-start.3 = (s32[10]{0:T(128)S(1)}, s32[10]{0:T(128)}, u32[]{:S(2)}) copy-start(s32[10]{0:T(128)} %constant.65.clone) | copy-start | bytes 124
  80.3 6.7 %copy-start.4 = (s32[10]{0:T(128)S(1)}, s32[10]{0:T(128)}, u32[]{:S(2)}) copy-start(s32[10]{0:T(128)} %constant.66.clone) | copy-start | bytes 124
  80.3 98.8 %all-to-all-start = ((bf16[16,1,32,2,4,512]{5,2,4,3,1,0:T(8,128)(2,1)}), bf16[16,1,32,2,4,512]{5,2,4,3,1,0:T(8,128)(2,1)}, u32[]{:S(2)}, u32[]{:S(2)}) async-start(bf16[16,1,32,2,4,512]{5,2,4,3,1,0:T(8,128)(2,1)} %fusion.12), calls=%async_computation | async-start | bytes 8388608 | tf_op jit(solution)/shard_map/all_to_all | solution.py:84
  220.8 2.3 copy-start
  224.9 5.6 %collective-permute-start = (f32[20,2,128,128]{3,2,1,0:T(8,128)}, f32[20,2,128,128]{3,2,1,0:T(8,128)S(1)}, u32[]{:S(2)}, u32[]{:S(2)}) collective-permute-start(f32[20,2,128,128]{3,2,1,0:T(8,128)} %constant_dynamic-slice_fusion), channel_id=1, source_target_pairs={{0,1},{1,0},{2,3},{3,2},{4,5},{5,4},{6,7},{7,6},{8,9},{9,8},{10,11... | collective-permute-start | bytes 7864328 | tf_op jit(solution)/shard_map/ppermute | solution.py:24
